TPU v7x, 32 devices: a whole 2x2x4 slice. The times are simulated.
32 devices in a mesh: grp: 2 (over x), rows: 8 (over z, y), cols: 2 (over core).
Axes of the slice: x: 2, y: 2, z: 4, core: 2. Of those that a mesh axis runs over, the one named last changes fastest.
Arguments:
- crop_feature_grid: bfloat16 [128, 256, 512], P(('grp', 'rows'), 'cols'), parts along dimension 0, may hold values from -6 to 6
- pixel_layernorm_gain: float32 [512], replicated, may hold values from 0.25 to 1.75
- triple_projection_matrix: bfloat16 [512, 1536], replicated, may hold values from -0.25 to 0.25
- halo_exit_matrix: bfloat16 [512, 512], replicated, may hold values from -0.25 to 0.25
- memory_slots: bfloat16 [256, 512], replicated, may hold values from -6 to 6
- memory_layernorm_gain: float32 [512], replicated, may hold values from 0.25 to 1.75
- memory_asking_matrix: bfloat16 [512, 512], replicated, may hold values from -0.25 to 0.25
- memory_exit_matrix: bfloat16 [512, 512], replicated, may hold values from -0.25 to 0.25
- branch_logit_multiplier: float32 [8], replicated, may hold values from 1 to 30, as said below
Outputs:
- tokens_out: bfloat16 [128, 256, 512], P(('grp', 'rows'), 'cols'), parts along dimension 0
- latent_mix: bfloat16 [512, 512], P('grp'), parts along dimension 0
There are 2 independent parts, one for each index of `grp`. A program takes and returns all parts, laid end to end along the dimension named above; an argument that names none is the same for every part. Nothing has to cross between parts.
Inputs may be any that keep to these rules, and one draw needn't show every extreme that they name: `branch_logit_multiplier`: a positive logit scale for each head.
All inputs are finite; a program needn't handle non-finite values.
Results may differ from a plain program's by a relative error of at most 0.0095.
The roundings to bfloat16 on the way count: a program that leaves them out, or rounds other values in their place, can miss the bound.
Values may be sent and summed in bfloat16 or wider, within the bound.
No kernel may reach another device: no remote copies, remote signals or barrier semaphores. Data moves between devices by JAX's collectives and lax.ppermute only.
A program may use at most 192 MiB of HBM per device.

v0:
```python
import math
import jax
import jax.numpy as jnp
from jax import lax
from jax.sharding import PartitionSpec as P

H = 8
BLK = 8
RIM = 3


def with_halo(array, sides, width):
    for axis, dim in sides:
        devices, length = (lax.axis_size(axis), array.shape[dim])
        up = [(i, (i + 1) % devices) for i in range(devices - 1)]
        down = [(j, i) for i, j in up]
        last = lax.slice_in_dim(array, length - width, length, axis=dim)
        initial = lax.slice_in_dim(array, 0, width, axis=dim)
        before = lax.ppermute(last, axis, up)
        after = lax.ppermute(initial, axis, down)
        array = jnp.concatenate([before, array, after], axis=dim)
    return array


def row_norm(values, gain_vector):
    floats = values.astype(jnp.float32)
    scaled = floats * lax.rsqrt(jnp.mean(floats * floats, axis=-1, keepdims=True) + 1e-05)
    return (scaled * gain_vector).astype(jnp.bfloat16)


def head_norm(floats, head_count):
    shaped = floats.reshape(floats.shape[:-1] + (head_count, floats.shape[-1] // head_count))
    normal = shaped * lax.rsqrt(jnp.mean(shaped * shaped, axis=-1, keepdims=True) + 1e-06)
    return normal.astype(jnp.bfloat16)


def halo_attention(queries, keys_ext, values_ext, inside, logit_divisor):
    rows_all, cols_all, head_count, channels_per_branch = queries.shape
    blocks_across = cols_all // BLK
    window = BLK + 2 * RIM
    offsets = (jnp.arange(blocks_across, dtype=jnp.int32) * BLK)[:, None] + jnp.arange(
        window, dtype=jnp.int32
    )[None, :]

    def one_row(block_row):
        query_blocks = queries.reshape(BLK, blocks_across, BLK, head_count, channels_per_branch)
        query_blocks = query_blocks.transpose(1, 0, 2, 3, 4).reshape(
            blocks_across, BLK * BLK, head_count, channels_per_branch
        )
        key_slab = keys_ext[:, offsets]
        key_blocks = key_slab.transpose(1, 0, 2, 3, 4).reshape(
            blocks_across, window * window, head_count, channels_per_branch
        )
        value_slab = values_ext[:, offsets]
        value_blocks = value_slab.transpose(1, 0, 2, 3, 4).reshape(
            blocks_across, window * window, head_count, channels_per_branch
        )
        mask_slab = inside[:, offsets]
        mask_blocks = mask_slab.transpose(1, 0, 2).reshape(blocks_across, window * window)
        scores = jnp.einsum(
            "bqhd,bkhd->bhqk", query_blocks, key_blocks, preferred_element_type=jnp.float32
        )
        scores = scores * logit_divisor[None, :, None, None]
        scores = jnp.where(mask_blocks[:, None, None, :], scores, -1e30)
        row_peak = jnp.max(scores, axis=-1, keepdims=True)
        expo = jnp.exp(scores - row_peak)
        row_total = jnp.sum(expo, axis=-1)
        weights = expo.astype(jnp.bfloat16)
        output = jnp.einsum(
            "bhqk,bkhd->bqhd", weights, value_blocks, preferred_element_type=jnp.float32
        )
        output = output / row_total.transpose(0, 2, 1)[..., None]
        output = output.reshape(
            blocks_across, BLK, BLK, head_count * channels_per_branch
        ).transpose(1, 0, 2, 3)
        return output.reshape(BLK, cols_all, head_count * channels_per_branch).astype(jnp.bfloat16)

    result = lax.map(one_row, jnp.arange(rows_all // BLK, dtype=jnp.int32))
    return result.reshape(rows_all, cols_all, head_count * channels_per_branch)


def per_device(
    crop_feature_grid,
    pixel_layernorm_gain,
    triple_projection_matrix,
    halo_exit_matrix,
    memory_slots,
    memory_layernorm_gain,
    memory_asking_matrix,
    memory_exit_matrix,
    branch_logit_multiplier,
):
    tile_rows, tile_cols, model_width = crop_feature_grid.shape
    head_count = H
    channels_per_branch = model_width // head_count
    normed = row_norm(crop_feature_grid, pixel_layernorm_gain)
    flat_normed = normed.reshape(-1, model_width)
    logit_divisor = branch_logit_multiplier / math.sqrt(channels_per_branch)
    projected = jnp.dot(flat_normed, triple_projection_matrix, preferred_element_type=jnp.float32)
    projected = projected.reshape(tile_rows, tile_cols, 3 * model_width)
    queries = head_norm(projected[..., :model_width], head_count)
    keys = head_norm(projected[..., model_width : 2 * model_width], head_count)
    values = (
        projected[..., 2 * model_width :]
        .reshape(tile_rows, tile_cols, head_count, channels_per_branch)
        .astype(jnp.bfloat16)
    )
    key_value = jnp.concatenate(
        [
            keys.reshape(tile_rows, tile_cols, model_width),
            values.reshape(tile_rows, tile_cols, model_width),
        ],
        axis=2,
    )
    key_value_ext = with_halo(key_value, (("rows", 0), ("cols", 1)), RIM)
    ext_rows, ext_cols = (key_value_ext.shape[0], key_value_ext.shape[1])
    keys_ext = key_value_ext[..., :model_width].reshape(
        ext_rows, ext_cols, head_count, channels_per_branch
    )
    values_ext = key_value_ext[..., model_width:].reshape(
        ext_rows, ext_cols, head_count, channels_per_branch
    )
    crop_rows = tile_rows * lax.axis_size("rows")
    crop_cols = tile_cols * lax.axis_size("cols")
    row_ids = (
        lax.axis_index("rows") * tile_rows - RIM + jnp.arange(tile_rows + 2 * RIM, dtype=jnp.int32)
    )
    col_ids = (
        lax.axis_index("cols") * tile_cols - RIM + jnp.arange(tile_cols + 2 * RIM, dtype=jnp.int32)
    )
    row_inside = (row_ids >= 0) & (row_ids < crop_rows)
    col_inside = (col_ids >= 0) & (col_ids < crop_cols)
    inside = row_inside[:, None] & col_inside[None, :]
    attended = halo_attention(queries, keys_ext, values_ext, inside, logit_divisor)
    branch = jnp.dot(
        attended.reshape(-1, model_width), halo_exit_matrix, preferred_element_type=jnp.float32
    )
    tokens_out = (
        crop_feature_grid.astype(jnp.float32) + branch.reshape(tile_rows, tile_cols, model_width)
    ).astype(jnp.bfloat16)
    latent_normed = row_norm(memory_slots, memory_layernorm_gain)
    latent_queries = head_norm(
        jnp.dot(latent_normed, memory_asking_matrix, preferred_element_type=jnp.float32), head_count
    )
    keys_heads = keys.reshape(-1, head_count, channels_per_branch).transpose(1, 0, 2)
    values_heads = values.reshape(-1, head_count, channels_per_branch).transpose(1, 0, 2)

    def one_head(operands):
        query_head, key_head, value_head, head_scale = operands
        scores = jnp.dot(query_head, key_head.T, preferred_element_type=jnp.float32) * head_scale
        row_peak = jnp.max(scores, axis=-1)
        expo = jnp.exp(scores - row_peak[:, None])
        row_total = jnp.sum(expo, axis=-1)
        weighted = jnp.dot(
            expo.astype(jnp.bfloat16), value_head, preferred_element_type=jnp.float32
        )
        return (row_peak, row_total, weighted)

    local_peak, local_total, local_sum = lax.map(
        one_head, (latent_queries.transpose(1, 0, 2), keys_heads, values_heads, logit_divisor)
    )
    crop_peak = lax.pmax(local_peak, ("rows", "cols"))
    factor = jnp.exp(local_peak - crop_peak)
    crop_total, crop_sum = lax.psum(
        (local_total * factor, local_sum * factor[..., None]), ("rows", "cols")
    )
    latent_heads = crop_sum / crop_total[..., None]
    latent_attended = latent_heads.transpose(1, 0, 2).reshape(-1, model_width).astype(jnp.bfloat16)
    latent_mix = jnp.dot(
        latent_attended, memory_exit_matrix, preferred_element_type=jnp.float32
    ).astype(jnp.bfloat16)
    return (tokens_out, latent_mix)


def solution(mesh):
    return jax.shard_map(
        per_device,
        mesh=mesh,
        in_specs=(P(("grp", "rows"), "cols", None), P(), P(), P(), P(), P(), P(), P(), P()),
        out_specs=(P(("grp", "rows"), "cols", None), P("grp", None)),
        check_vma=False,
    )
```

profile of v0, /device:TPU:0, one launch (start us, length us, event | category | flops | bytes accessed | tf_op | source)
XLA Modules:
  0.0 278.7 jit_solution(9625256363272125825)
XLA Ops:
  8.9 3.1 %fusion.33 = f32[8,128,1536]{2,1,0:T(8,128)S(1)} fusion(bf16[512,1536]{1,0:T(8,128)(2,1)S(1)} %copy-done, bf16[8,128,512]{2,1,0:T(8,128)(2,1)} %param.11, f32[512]{0:T(512)} %param.12, f32[8,128]{1,0:T(8,128)S(1)} %add_rsqrt_fusion.3), kind=kOutput, calls=%fused_computation.50 | convolution fusion | flops 1612709888 | bytes 8919040 | tf_op jit(solution)/shard_map/dot_general | solution.py:99
  12.0 4.1 %fusion.58 = (f32[8,128,512]{2,1,0:T(8,128)}, f32[8,128,512]{2,1,0:T(8,128)}, f32[8,128,512]{2,1,0:T(8,128)}, f32[8,128,512]{2,1,0:T(8,128)}) fusion(f32[8,128,1536]{2,1,0:T(8,128)S(1)} %fusion.33), kind=kLoop, calls=%fused_computation.97 | loop fusion | flops 1048576 | bytes 12582912 | tf_op jit(solution)/shard_map/slice | solution.py:102
  17.4 2.9 %copy.38 = f32[8,128,512]{1,2,0:T(8,128)} copy(f32[8,128,512]{2,1,0:T(8,128)} %get-tuple-element.110) | data formatting | bytes 4194304 | tf_op jit(solution)/shard_map/mul | solution.py:33
  22.1 2.9 %copy.52 = f32[8,128,512]{1,0,2:T(8,128)} copy(f32[8,128,512]{2,1,0:T(8,128)} %get-tuple-element.109) | data formatting | bytes 4194304 | tf_op jit(solution)/shard_map/slice | solution.py:102
  32.4 32.1 %while.4 = (s32[]{:T(128)}, f32[8,256]{1,0:T(8,128)S(1)}, f32[8,256]{1,0:T(8,128)S(1)}, f32[8,256,64]{1,2,0:T(8,128)}, bf16[8,256,64]{1,2,0:T(8,128)(2,1)S(1)}, ...) while((s32[]{:T(128)}, f32[8,256]{1,0:T(8,128)S(1)}, ...), condition=%wide.region_10.11_spmd, body=%wide.region_7.0_spmd.sunk | while | flops 68681216 | bytes 3517049 | solution.py:159
  64.5 35.4 %pmax.7 = f32[8,256]{1,0:T(8,128)S(1)} all-reduce(f32[8,256]{1,0:T(8,128)S(1)} %get-tuple-element.71), channel_id=1, replica_groups=mesh['grp'=2,'rows'=8,'cols'=2] {'rows','cols'}, use_global_device_ids=true, to_apply=%region_11.12 | all-reduce | flops 2048 | bytes 16384 | tf_op jit(solution)/shard_map/pmax | solution.py:162
  113.1 4.4 %reshape.188 = f32[8,16,8,8,64]{4,3,2,1,0:T(8,128)} reshape(f32[8,128,512]{2,1,0:T(8,128)} %get-tuple-element.112) | data formatting | bytes 4194304 | tf_op jit(solution)/shard_map/reshape | solution.py:32
  117.4 2.9 %copy.43 = f32[8,128,512]{1,2,0:T(8,128)} copy(f32[8,128,512]{2,1,0:T(8,128)} %get-tuple-element.111) | data formatting | bytes 4194304 | tf_op jit(solution)/shard_map/mul | solution.py:33
  124.5 40.9 %psum.15 = f32[8,256]{1,0:T(8,128)S(1)} all-reduce(f32[8,256]{1,0:T(8,128)S(1)} %get-tuple-element.105), channel_id=1, replica_groups=mesh['grp'=2,'rows'=8,'cols'=2] {'rows','cols'}, use_global_device_ids=true, to_apply=%region_13.14 | all-reduce | flops 2048 | bytes 16384 | tf_op jit(solution)/shard_map/psum | solution.py:164
  165.5 3.9 %fusion.30 = bf16[16,8,8,8,64]{4,3,2,0,1:T(8,128)(2,1)} fusion(f32[8,16,8,8,64]{4,3,2,1,0:T(8,128)} %reshape.188, f32[8,16,8,8]{3,2,1,0:T(8,128)} %bitcast.109), kind=kLoop, calls=%fused_computation.42 | loop fusion | flops 1048576 | bytes 3178496 | tf_op jit(solution)/shard_map/while/body/eval_jaxpr/transpose | solution.py:47
  169.4 26.6 %all-reduce.2.cloned.1.call-done = f32[8,256,64]{1,2,0:T(8,128)} async-done(((f32[8,256,64]{1,2,0:T(8,128)}), f32[8,256,64]{1,2,0:T(8,128)}) %all-reduce.2.cloned.1.call-update) | async-done | bytes 524304 | tf_op jit(solution)/shard_map/psum | solution.py:164
  203.7 3.6 %pad_maximum_fusion = bf16[14,134,1024]{2,1,0:T(8,128)(2,1)S(1)} fusion(bf16[14,3,1024]{2,1,0:T(4,128)(2,1)S(1)} %collective-permute-done.3, bf16[3,128,1024]{2,1,0:T(8,128)(2,1)} %collective-permute-done.1, bf16[8,128,512]{2,1,0:T(8,128)(2,1)S(1)} %slice.51, bf16[8,128,512]{2,1,0:T(8,128)(2,1)S(1)} %multiply_convert_fusion.2, ...), kind=kLoop, calls=%fused_computation.34 | loop fusion | flops 23052288 | bytes 7684096 | tf_op jit(solution)/shard_map/concatenate | solution.py:21
  208.9 5.6 %reshape.190 = bf16[14,134,8,64]{3,2,1,0:T(8,128)(2,1)} reshape(bf16[14,134,512]{2,1,0:T(8,128)(2,1)} %get-tuple-element.114) | data formatting | bytes 3842048 | tf_op jit(solution)/shard_map/reshape | solution.py:117
  214.5 7.1 %gather_fusion.2 = bf16[224,14,8,64]{3,2,1,0:T(8,128)(2,1)} fusion(bf16[14,134,8,64]{3,2,1,0:T(8,128)(2,1)} %reshape.190, s32[1024]{0:T(1024)S(1)} %pad_clamp_fusion), kind=kCustom, calls=%fused_computation.2 | custom fusion | bytes 6423424 | tf_op jit(solution)/shard_map/while/body/eval_jaxpr/gather | solution.py:50
  221.5 6.6 %copy.46 = bf16[16,14,14,8,64]{4,3,1,2,0:T(8,128)(2,1)} copy(bf16[16,14,14,8,64]{4,3,2,1,0:T(8,128)(2,1)} %bitcast.104) | data formatting | bytes 6422528 | tf_op jit(solution)/shard_map/while/body/eval_jaxpr/gather | solution.py:50
  228.2 3.3 %reshape.186 = bf16[14,134,8,64]{3,2,1,0:T(8,128)(2,1)} reshape(bf16[14,134,512]{2,1,0:T(8,128)(2,1)S(1)} %get-tuple-element.113) | data formatting | bytes 3842048 | tf_op jit(solution)/shard_map/reshape | solution.py:120
  231.5 7.0 %gather_fusion = bf16[224,14,8,64]{3,2,1,0:T(8,128)(2,1)} fusion(bf16[14,134,8,64]{3,2,1,0:T(8,128)(2,1)} %reshape.186, s32[1024]{0:T(1024)S(1)} %pad_clamp_fusion), kind=kCustom, calls=%fused_computation | custom fusion | bytes 6423424 | tf_op jit(solution)/shard_map/while/body/eval_jaxpr/gather | solution.py:54
  238.5 6.8 %copy.40 = bf16[16,14,14,8,64]{4,3,1,2,0:T(8,128)(2,1)} copy(bf16[16,14,14,8,64]{4,3,2,1,0:T(8,128)(2,1)} %bitcast.103) | data formatting | bytes 6422528 | tf_op jit(solution)/shard_map/while/body/eval_jaxpr/gather | solution.py:54
  245.3 6.5 %fusion.13 = (f32[16,8,64]{2,1,0:T(8,128)S(1)}, f32[16,8,64,196]{3,2,1,0:T(8,128)S(1)}) fusion(f32[8]{0:T(128)S(1)} %get-tuple-element.217, pred[16,196]{1,0:T(8,128)(4,1)S(1)} %broadcast_in_dim.60, bf16[16,196,8,64]{3,2,1,0:T(8,128)(2,1)} %bitcast.106, bf16[16,8,8,8,64]{4,3,2,0,1:T(8,128)(2,1)S(1)} %copy-done.4), kind=kOutput, calls=%fused_computation.20 | convolution fusion | flops 210329600 | bytes 10718304 | tf_op jit(solution)/shard_map/while/body/eval_jaxpr/bqhd,bkhd->bhqk/dot_general | solution.py:60
  251.8 3.7 %fusion.18 = f32[16,8,64]{2,1,0:T(8,128)S(1)} fusion(f32[16,8,64,196]{3,2,1,0:T(8,128)S(1)} %get-tuple-element.122, f32[16,8,64]{2,1,0:T(8,128)S(1)} %get-tuple-element.121, f32[8]{0:T(128)S(1)} %get-tuple-element.217, pred[16,196]{1,0:T(8,128)(4,1)S(1)} %broadcast_in_dim.60), kind=kLoop, calls=%fused_computation.25 | loop fusion | flops 6414336 | bytes 6491232 | tf_op jit(solution)/shard_map/while/body/eval_jaxpr/reduce_sum | solution.py:67
  255.5 6.0 %fusion.21 = bf16[16,64,8,64]{1,3,2,0:T(8,128)(2,1)} fusion(f32[16,64,8]{1,2,0:T(8,128)S(1)} %bitcast.114, f32[16,8,64,196]{3,2,1,0:T(8,128)S(1)} %get-tuple-element.122, f32[16,8,64]{2,1,0:T(8,128)S(1)} %get-tuple-element.121, f32[8]{0:T(128)S(1)} %get-tuple-element.217, pred[16,196]{1,0:T(8,128)(4,1)S(1)} %broadcast_in_dim.60, ...), kind=kOutput, calls=%fused_computation.28 | convolution fusion | flops 212992000 | bytes 10751072 | tf_op jit(solution)/shard_map/while/body/eval_jaxpr/bhqk,bkhd->bqhd/dot_general | solution.py:69
  261.5 4.3 %copy.49 = bf16[16,64,8,64]{3,2,1,0:T(8,128)(2,1)} copy(bf16[16,64,8,64]{1,3,2,0:T(8,128)(2,1)} %fusion.21) | data formatting | bytes 2097152 | tf_op jit(solution)/shard_map/while/body/eval_jaxpr/convert_element_type | solution.py:76
  265.8 3.2 %convert_element_type.79 = bf16[16,8,8,512]{3,2,1,0:T(8,128)(2,1)S(1)} reshape(bf16[16,64,8,64]{3,2,1,0:T(8,128)(2,1)} %copy.49) | data formatting | bytes 2097152 | tf_op jit(solution)/shard_map/while/body/eval_jaxpr/convert_element_type | solution.py:76
  269.0 2.9 %fusion.29 = bf16[8,128,512]{2,1,0:T(8,128)(2,1)} fusion(bf16[8,128,512]{2,1,0:T(8,128)(2,1)} %param.11, bf16[512,512]{1,0:T(8,128)(2,1)S(1)} %copy-done.9, bf16[16,8,8,512]{3,2,1,0:T(8,128)(2,1)S(1)} %convert_element_type.79), kind=kOutput, calls=%fused_computation.41 | convolution fusion | flops 538443776 | bytes 3670016 | tf_op jit(solution)/shard_map/dot_general | solution.py:135
  (123 shorter events, 70.3 us)
Async XLA Ops:
  7.2 1.7 copy-start
  7.2 188.8 %all-reduce.2.cloned.1.call-start = ((), (), s32[]{:S(2)}) async-start(), calls=%async_computation | async-start | bytes 1048576 | tf_op jit(solution)/shard_map/psum | solution.py:164
  12.0 5.2 %copy-start.2 = (f32[8,128,1536]{2,1,0:T(8,128)}, f32[8,128,1536]{2,1,0:T(8,128)S(1)}, u32[]{:S(2)}) copy-start(f32[8,128,1536]{2,1,0:T(8,128)S(1)} %fusion.33) | copy-start | bytes 18874372
  25.1 4.8 %copy-start.10 = (f32[8]{0:T(128)S(1)}, f32[8]{0:T(128)}, u32[]{:S(2)}) copy-start(f32[8]{0:T(128)} %param.19) | copy-start | bytes 100
  25.1 4.8 %copy-start.5 = (bf16[256,512]{1,0:T(8,128)(2,1)S(1)}, bf16[256,512]{1,0:T(8,128)(2,1)}, u32[]{:S(2)}) copy-start(bf16[256,512]{1,0:T(8,128)(2,1)} %param.15) | copy-start | bytes 786436
  25.1 5.0 %copy-start.6 = (bf16[512,512]{1,0:T(8,128)(2,1)S(1)}, bf16[512,512]{1,0:T(8,128)(2,1)}, u32[]{:S(2)}) copy-start(bf16[512,512]{1,0:T(8,128)(2,1)} %param.17) | copy-start | bytes 1572868
  25.1 5.0 %copy-start.8 = (f32[512]{0:T(512)S(1)}, f32[512]{0:T(512)}, u32[]{:S(2)}) copy-start(f32[512]{0:T(512)} %param.16) | copy-start | bytes 6148
  110.2 86.9 %collective-permute-start = (bf16[3,128,1024]{2,1,0:T(8,128)(2,1)}, bf16[3,128,1024]{2,1,0:T(8,128)(2,1)S(1)}, u32[]{:S(2)}, u32[]{:S(2)}) collective-permute-start(bf16[3,128,1024]{2,1,0:T(8,128)(2,1)} %get-tuple-element.117), channel_id=1, source_target_pairs={{0,2},{2,4},{4,6},{6,8},{8,10},{10,12},{12,14},{1,3},{3,5},{5,7},{... | collective-permute-start | bytes 2359304 | tf_op jit(solution)/shard_map/ppermute | solution.py:19
  111.6 85.6 %collective-permute-start.1 = (bf16[3,128,1024]{2,1,0:T(8,128)(2,1)}, bf16[3,128,1024]{2,1,0:T(8,128)(2,1)}, u32[]{:S(2)}, u32[]{:S(2)}) collective-permute-start(bf16[3,128,1024]{2,1,0:T(8,128)(2,1)} %get-tuple-element.118), channel_id=1, source_target_pairs={{2,0},{4,2},{6,4},{8,6},{10,8},{12,10},{14,12},{3,1},{5,3},{7,5},{... | collective-permute-start | bytes 2359304 | tf_op jit(solution)/shard_map/ppermute | solution.py:20
  196.0 6.0 %copy-start.7 = (bf16[512,512]{1,0:T(8,128)(2,1)S(1)}, bf16[512,512]{1,0:T(8,128)(2,1)}, u32[]{:S(2)}) copy-start(bf16[512,512]{1,0:T(8,128)(2,1)} %param.18) | copy-start | bytes 1572868
  198.1 4.9 %collective-permute-start.2 = (bf16[14,3,1024]{2,1,0:T(4,128)(2,1)S(1)}, bf16[14,3,1024]{2,1,0:T(4,128)(2,1)S(1)}, u32[]{:S(2)}, u32[]{:S(2)}) collective-permute-start(bf16[14,3,1024]{2,1,0:T(4,128)(2,1)S(1)} %get-tuple-element.115), channel_id=1, source_target_pairs={{0,1},{2,3},{4,5},{6,7},{8,9},{10,11},{12,13},{14,15},{16,17},{18,... | collective-permute-start | bytes 258056 | tf_op jit(solution)/shard_map/ppermute | solution.py:19
  200.4 3.2 %collective-permute-start.3 = (bf16[14,3,1024]{2,1,0:T(4,128)(2,1)S(1)}, bf16[14,3,1024]{2,1,0:T(4,128)(2,1)S(1)}, u32[]{:S(2)}, u32[]{:S(2)}) collective-permute-start(bf16[14,3,1024]{2,1,0:T(4,128)(2,1)S(1)} %get-tuple-element.116), channel_id=1, source_target_pairs={{1,0},{3,2},{5,4},{7,6},{9,8},{11,10},{13,12},{15,14},{17,16},{19,... | collective-permute-start | bytes 258056 | tf_op jit(solution)/shard_map/ppermute | solution.py:20
  238.5 6.8 %copy-start.4 = (bf16[16,8,8,8,64]{4,3,2,0,1:T(8,128)(2,1)S(1)}, bf16[16,8,8,8,64]{4,3,2,0,1:T(8,128)(2,1)}, u32[]{:S(2)}) copy-start(bf16[16,8,8,8,64]{4,3,2,0,1:T(8,128)(2,1)} %fusion.30) | copy-start | bytes 3145732
  251.8 3.7 %copy-start.3 = (bf16[16,14,14,8,64]{4,3,1,2,0:T(8,128)(2,1)S(1)}, bf16[16,14,14,8,64]{4,3,1,2,0:T(8,128)(2,1)}, u32[]{:S(2)}) copy-start(bf16[16,14,14,8,64]{4,3,1,2,0:T(8,128)(2,1)} %copy.40) | copy-start | bytes 9633796
  261.5 7.5 %copy-start.9 = (bf16[512,512]{1,0:T(8,128)(2,1)S(1)}, bf16[512,512]{1,0:T(8,128)(2,1)}, u32[]{:S(2)}) copy-start(bf16[512,512]{1,0:T(8,128)(2,1)} %param.14) | copy-start | bytes 1572868
  261.5 10.4 %copy-start.1 = (bf16[512,1536]{1,0:T(8,128)(2,1)S(1)}, bf16[512,1536]{1,0:T(8,128)(2,1)}, u32[]{:S(2)}) copy-start(bf16[512,1536]{1,0:T(8,128)(2,1)} %param.13) | copy-start | bytes 4718596
Sparse Core Ops, SparseCore 0:
  102.0 93.8 all-reduce.1
where the time goes:
time: 280 us; the launch traced here: 279 us
  local copies, waits for them, and re-layouts  77.1 us (28%)
  blocking collectives  76.4 us (27%)
  matrix products  43.6 us (16%)
  other arithmetic  33.2 us (12%)
  waiting for transfers between devices  27.3 us (10%)
  between operations  14.4 us (5%)
  starting transfers between devices  6.5 us (2%)
    psum x1, blocking collectives, per_device(): lax.psum((local_total * factor, local_sum * factor[..., None]), ('rows',...  40.9 us
    pmax x1, blocking collectives, per_device(): crop_peak = lax.pmax(local_peak, ('rows', 'cols'))  35.4 us
    psum x1, waiting for transfers between devices, per_device(): lax.psum((local_total * factor, local_sum * factor[..., None]), ('rows',...  26.6 us
    dot_general x8, matrix products, one_head(): jnp.dot(expo.astype(jnp.bfloat16), value_head, preferred_element_type=jnp...  15.1 us
    gather x2, local copies, waits for them, and re-layouts, one_row(): value_slab = values_ext[:, offsets]  13.8 us
    gather x2, local copies, waits for them, and re-layouts, one_row(): key_slab = keys_ext[:, offsets]  13.7 us
    dot_general x8, matrix products, one_head(): jnp.dot(query_head, key_head.T, preferred_element_type=jnp.float32)  8.53 us
    convert_element_type x2, local copies, waits for them, and re-layouts, one_row(): output.reshape(BLK, cols_all, head_count * channels_per_branch)  7.46 us
  transfers between devices with their start and end apart: 5, of which 2 were waited for; matrix products, arithmetic and copies ran while one was open for 9% of the time, Pallas kernels for 0%

commit v1 on v0

--- a/solution.py
+++ b/solution.py
@@ -7,6 +7,12 @@
 H = 8
 BLK = 8
 RIM = 3
+
+
+def fill_strips_all(net_axis, axis_id, z_in):
+    for ix in (net_axis, axis_id):
+        z_in = lax.psum(z_in, axis_name=ix)
+    return z_in
 
 
 def with_halo(array, sides, width):
@@ -161,8 +167,8 @@
     )
     crop_peak = lax.pmax(local_peak, ("rows", "cols"))
     factor = jnp.exp(local_peak - crop_peak)
-    crop_total, crop_sum = lax.psum(
-        (local_total * factor, local_sum * factor[..., None]), ("rows", "cols")
+    crop_total, crop_sum = fill_strips_all(
+        "cols", axis_id="rows", z_in=(local_total * factor, local_sum * factor[..., None])
     )
     latent_heads = crop_sum / crop_total[..., None]
     latent_attended = latent_heads.transpose(1, 0, 2).reshape(-1, model_width).astype(jnp.bfloat16)

time: 280 us -> 251 us (0.90)
  blocking collectives: 76.4 us -> 58.7 us
  waiting for transfers between devices: 27.3 us -> 16.8 us
    psum x1 -> x2, waiting for transfers between devices: 26.6 us -> 1.21 us  [fill_strips_all(): z_in = lax.psum(z_in, axis_name=ix)]
    psum x1 -> x2, blocking collectives: 40.9 us -> 23.2 us  [fill_strips_all(): z_in = lax.psum(z_in, axis_name=ix)]
    ppermute x2, waiting for transfers between devices: 0.01 us -> 15.5 us  [with_halo(): before = lax.ppermute(last, axis, up)]
  transfers between devices with their start and end apart: 5 -> 6, of which waited for: 2 -> 2; matrix products, arithmetic and copies ran while one was open for 9% -> 37% of each run, Pallas kernels for 0% -> 0%
where the time goes in v1:
time: 251 us; the launch traced here: 249 us
  local copies, waits for them, and re-layouts  76.6 us (31%)
  blocking collectives  58.7 us (23%)
  matrix products  43.8 us (17%)
  other arithmetic  33.1 us (13%)
  waiting for transfers between devices  16.8 us (7%)
  between operations  14.4 us (6%)
  starting transfers between devices  5.73 us (2%)
    pmax x1, blocking collectives, per_device(): crop_peak = lax.pmax(local_peak, ('rows', 'cols'))  35.4 us
    psum x2, blocking collectives, fill_strips_all(): z_in = lax.psum(z_in, axis_name=ix)  23.2 us
    ppermute x2, waiting for transfers between devices, with_halo(): before = lax.ppermute(last, axis, up)  15.5 us
    dot_general x8, matrix products, one_head(): jnp.dot(expo.astype(jnp.bfloat16), value_head, preferred_element_type=jnp...  15.1 us
    gather x2, local copies, waits for them, and re-layouts, one_row(): value_slab = values_ext[:, offsets]  13.8 us
    gather x2, local copies, waits for them, and re-layouts, one_row(): key_slab = keys_ext[:, offsets]  13.8 us
    dot_general x8, matrix products, one_head(): jnp.dot(query_head, key_head.T, preferred_element_type=jnp.float32)  8.53 us
    convert_element_type x2, local copies, waits for them, and re-layouts, one_row(): output.reshape(BLK, cols_all, head_count * channels_per_branch)  7.5 us
  transfers between devices with their start and end apart: 6, of which 2 were waited for; matrix products, arithmetic and copies ran while one was open for 37% of the time, Pallas kernels for 0%

profile of v1, /device:TPU:0, one launch (start us, length us, event | category | flops | bytes accessed | tf_op | source)
XLA Modules:
  0.0 249.4 jit_solution(1173466186649939139)
XLA Ops:
  8.9 3.1 %fusion.33 = f32[8,128,1536]{2,1,0:T(8,128)S(1)} fusion(bf16[512,1536]{1,0:T(8,128)(2,1)S(1)} %copy-done, bf16[8,128,512]{2,1,0:T(8,128)(2,1)} %param.11, f32[512]{0:T(512)} %param.12, f32[8,128]{1,0:T(8,128)S(1)} %add_rsqrt_fusion.3), kind=kOutput, calls=%fused_computation.50 | convolution fusion | flops 1612709888 | bytes 8919040 | tf_op jit(solution)/shard_map/dot_general | solution.py:105
  12.0 4.1 %fusion.58 = (f32[8,128,512]{2,1,0:T(8,128)}, f32[8,128,512]{2,1,0:T(8,128)}, f32[8,128,512]{2,1,0:T(8,128)}, f32[8,128,512]{2,1,0:T(8,128)}) fusion(f32[8,128,1536]{2,1,0:T(8,128)S(1)} %fusion.33), kind=kLoop, calls=%fused_computation.97 | loop fusion | flops 1048576 | bytes 12582912 | tf_op jit(solution)/shard_map/slice | solution.py:108
  22.3 2.9 %copy.52 = f32[8,128,512]{1,0,2:T(8,128)} copy(f32[8,128,512]{2,1,0:T(8,128)} %get-tuple-element.109) | data formatting | bytes 4194304 | tf_op jit(solution)/shard_map/slice | solution.py:108
  32.5 32.1 %while.4 = (s32[]{:T(128)}, f32[8,256]{1,0:T(8,128)S(1)}, f32[8,256]{1,0:T(8,128)S(1)}, f32[8,256,64]{1,2,0:T(8,128)}, bf16[8,256,64]{1,2,0:T(8,128)(2,1)S(1)}, ...) while((s32[]{:T(128)}, f32[8,256]{1,0:T(8,128)S(1)}, ...), condition=%wide.region_10.11_spmd, body=%wide.region_7.0_spmd.sunk | while | flops 68681216 | bytes 3517049 | solution.py:165
  64.6 35.4 %pmax.7 = f32[8,256]{1,0:T(8,128)S(1)} all-reduce(f32[8,256]{1,0:T(8,128)S(1)} %get-tuple-element.71), channel_id=1, replica_groups=mesh['grp'=2,'rows'=8,'cols'=2] {'rows','cols'}, use_global_device_ids=true, to_apply=%region_11.12 | all-reduce | flops 2048 | bytes 16384 | tf_op jit(solution)/shard_map/pmax | solution.py:168
  113.2 3.0 %copy.43 = f32[8,128,512]{1,2,0:T(8,128)} copy(f32[8,128,512]{2,1,0:T(8,128)} %get-tuple-element.111) | data formatting | bytes 4194304 | tf_op jit(solution)/shard_map/mul | solution.py:39
  118.2 4.4 %reshape.188 = f32[8,16,8,8,64]{4,3,2,1,0:T(8,128)} reshape(f32[8,128,512]{2,1,0:T(8,128)} %get-tuple-element.112) | data formatting | bytes 4194304 | tf_op jit(solution)/shard_map/reshape | solution.py:38
  122.7 3.8 %fusion.30 = bf16[16,8,8,8,64]{4,3,2,0,1:T(8,128)(2,1)} fusion(f32[8,16,8,8,64]{4,3,2,1,0:T(8,128)} %reshape.188, f32[8,16,8,8]{3,2,1,0:T(8,128)S(1)} %bitcast.109), kind=kLoop, calls=%fused_computation.42 | loop fusion | flops 1048576 | bytes 3178496 | tf_op jit(solution)/shard_map/while/body/eval_jaxpr/transpose | solution.py:53
  126.6 15.5 %collective-permute-done = bf16[3,128,1024]{2,1,0:T(8,128)(2,1)S(1)} collective-permute-done((bf16[3,128,1024]{2,1,0:T(8,128)(2,1)}, bf16[3,128,1024]{2,1,0:T(8,128)(2,1)S(1)}, u32[]{:S(2)}, u32[]{:S(2)}) %collective-permute-start) | collective-permute-done | bytes 786464 | tf_op jit(solution)/shard_map/ppermute | solution.py:25
  147.3 3.3 %psum.30 = f32[8,256]{1,0:T(8,128)S(1)} all-reduce(f32[8,256]{1,0:T(8,128)S(1)} %get-tuple-element.105), channel_id=1, replica_groups=mesh['grp'=2,'rows'=8,'cols'=2] {'cols'}, use_global_device_ids=true, to_apply=%region_14.15 | all-reduce | flops 2048 | bytes 16384 | tf_op jit(solution)/shard_map/psum | solution.py:14
  150.6 19.9 %psum.31 = f32[8,256]{1,0:T(8,128)S(1)} all-reduce(f32[8,256]{1,0:T(8,128)S(1)} %psum.30), channel_id=1, replica_groups=mesh['grp'=2,'rows'=8,'cols'=2] {'rows'}, use_global_device_ids=true, to_apply=%region_15.16 | all-reduce | flops 2048 | bytes 16384 | tf_op jit(solution)/shard_map/psum | solution.py:14
  170.6 3.6 %pad_maximum_fusion = bf16[14,134,1024]{2,1,0:T(8,128)(2,1)S(1)} fusion(bf16[14,3,1024]{2,1,0:T(4,128)(2,1)S(1)} %collective-permute-done.3, bf16[3,128,1024]{2,1,0:T(8,128)(2,1)} %collective-permute-done.1, bf16[8,128,512]{2,1,0:T(8,128)(2,1)S(1)} %slice.51, bf16[8,128,512]{2,1,0:T(8,128)(2,1)S(1)} %multiply_convert_fusion.2, ...), kind=kLoop, calls=%fused_computation.34 | loop fusion | flops 23052288 | bytes 7684096 | tf_op jit(solution)/shard_map/concatenate | solution.py:27
  175.8 5.6 %reshape.190 = bf16[14,134,8,64]{3,2,1,0:T(8,128)(2,1)} reshape(bf16[14,134,512]{2,1,0:T(8,128)(2,1)} %get-tuple-element.114) | data formatting | bytes 3842048 | tf_op jit(solution)/shard_map/reshape | solution.py:123
  181.5 7.1 %gather_fusion.2 = bf16[224,14,8,64]{3,2,1,0:T(8,128)(2,1)} fusion(bf16[14,134,8,64]{3,2,1,0:T(8,128)(2,1)} %reshape.190, s32[1024]{0:T(1024)S(1)} %pad_clamp_fusion), kind=kCustom, calls=%fused_computation.2 | custom fusion | bytes 6423424 | tf_op jit(solution)/shard_map/while/body/eval_jaxpr/gather | solution.py:56
  188.6 6.7 %copy.46 = bf16[16,14,14,8,64]{4,3,1,2,0:T(8,128)(2,1)} copy(bf16[16,14,14,8,64]{4,3,2,1,0:T(8,128)(2,1)} %bitcast.104) | data formatting | bytes 6422528 | tf_op jit(solution)/shard_map/while/body/eval_jaxpr/gather | solution.py:56
  195.2 3.3 %reshape.186 = bf16[14,134,8,64]{3,2,1,0:T(8,128)(2,1)} reshape(bf16[14,134,512]{2,1,0:T(8,128)(2,1)S(1)} %get-tuple-element.113) | data formatting | bytes 3842048 | tf_op jit(solution)/shard_map/reshape | solution.py:126
  198.6 7.0 %gather_fusion = bf16[224,14,8,64]{3,2,1,0:T(8,128)(2,1)} fusion(bf16[14,134,8,64]{3,2,1,0:T(8,128)(2,1)} %reshape.186, s32[1024]{0:T(1024)S(1)} %pad_clamp_fusion), kind=kCustom, calls=%fused_computation | custom fusion | bytes 6423424 | tf_op jit(solution)/shard_map/while/body/eval_jaxpr/gather | solution.py:60
  205.6 6.8 %copy.40 = bf16[16,14,14,8,64]{4,3,1,2,0:T(8,128)(2,1)} copy(bf16[16,14,14,8,64]{4,3,2,1,0:T(8,128)(2,1)} %bitcast.103) | data formatting | bytes 6422528 | tf_op jit(solution)/shard_map/while/body/eval_jaxpr/gather | solution.py:60
  212.4 6.5 %fusion.13 = (f32[16,8,64]{2,1,0:T(8,128)S(1)}, f32[16,8,64,196]{3,2,1,0:T(8,128)S(1)}) fusion(f32[8]{0:T(128)S(1)} %get-tuple-element.221, pred[16,196]{1,0:T(8,128)(4,1)S(1)} %broadcast_in_dim.60, bf16[16,196,8,64]{3,2,1,0:T(8,128)(2,1)} %bitcast.106, bf16[16,8,8,8,64]{4,3,2,0,1:T(8,128)(2,1)S(1)} %copy-done.4), kind=kOutput, calls=%fused_computation.20 | convolution fusion | flops 210329600 | bytes 10718304 | tf_op jit(solution)/shard_map/while/body/eval_jaxpr/bqhd,bkhd->bhqk/dot_general | solution.py:66
  218.9 3.7 %fusion.18 = f32[16,8,64]{2,1,0:T(8,128)S(1)} fusion(f32[16,8,64,196]{3,2,1,0:T(8,128)S(1)} %get-tuple-element.122, f32[16,8,64]{2,1,0:T(8,128)S(1)} %get-tuple-element.121, f32[8]{0:T(128)S(1)} %get-tuple-element.221, pred[16,196]{1,0:T(8,128)(4,1)S(1)} %broadcast_in_dim.60), kind=kLoop, calls=%fused_computation.25 | loop fusion | flops 6414336 | bytes 6491232 | tf_op jit(solution)/shard_map/while/body/eval_jaxpr/reduce_sum | solution.py:73
  222.6 6.0 %fusion.21 = bf16[16,64,8,64]{1,3,2,0:T(8,128)(2,1)} fusion(f32[16,64,8]{1,2,0:T(8,128)S(1)} %bitcast.114, f32[16,8,64,196]{3,2,1,0:T(8,128)S(1)} %get-tuple-element.122, f32[16,8,64]{2,1,0:T(8,128)S(1)} %get-tuple-element.121, f32[8]{0:T(128)S(1)} %get-tuple-element.221, pred[16,196]{1,0:T(8,128)(4,1)S(1)} %broadcast_in_dim.60, ...), kind=kOutput, calls=%fused_computation.28 | convolution fusion | flops 212992000 | bytes 10751072 | tf_op jit(solution)/shard_map/while/body/eval_jaxpr/bhqk,bkhd->bqhd/dot_general | solution.py:75
  228.6 4.2 %copy.49 = bf16[16,64,8,64]{3,2,1,0:T(8,128)(2,1)} copy(bf16[16,64,8,64]{1,3,2,0:T(8,128)(2,1)} %fusion.21) | data formatting | bytes 2097152 | tf_op jit(solution)/shard_map/while/body/eval_jaxpr/convert_element_type | solution.py:82
  232.9 3.2 %convert_element_type.79 = bf16[16,8,8,512]{3,2,1,0:T(8,128)(2,1)S(1)} reshape(bf16[16,64,8,64]{3,2,1,0:T(8,128)(2,1)} %copy.49) | data formatting | bytes 2097152 | tf_op jit(solution)/shard_map/while/body/eval_jaxpr/convert_element_type | solution.py:82
  236.1 3.1 %fusion.29 = bf16[8,128,512]{2,1,0:T(8,128)(2,1)} fusion(bf16[8,128,512]{2,1,0:T(8,128)(2,1)} %param.11, bf16[512,512]{1,0:T(8,128)(2,1)} %param.14, bf16[16,8,8,512]{3,2,1,0:T(8,128)(2,1)S(1)} %convert_element_type.79), kind=kOutput, calls=%fused_computation.41 | convolution fusion | flops 538443776 | bytes 3670016 | tf_op jit(solution)/shard_map/dot_general | solution.py:141
  (125 shorter events, 72.3 us)
Async XLA Ops:
  7.2 1.7 copy-start
  7.2 163.4 %all-reduce.3.cloned.1.call-start = ((), (), s32[]{:S(2)}) async-start(), calls=%async_computation | async-start | bytes 1048576 | tf_op jit(solution)/shard_map/psum | solution.py:14
  12.0 5.3 %copy-start.2 = (f32[8,128,1536]{2,1,0:T(8,128)}, f32[8,128,1536]{2,1,0:T(8,128)S(1)}, u32[]{:S(2)}) copy-start(f32[8,128,1536]{2,1,0:T(8,128)S(1)} %fusion.33) | copy-start | bytes 18874372
  25.2 4.8 %copy-start.9 = (f32[8]{0:T(128)S(1)}, f32[8]{0:T(128)}, u32[]{:S(2)}) copy-start(f32[8]{0:T(128)} %param.19) | copy-start | bytes 100
  25.2 4.8 %copy-start.5 = (bf16[256,512]{1,0:T(8,128)(2,1)S(1)}, bf16[256,512]{1,0:T(8,128)(2,1)}, u32[]{:S(2)}) copy-start(bf16[256,512]{1,0:T(8,128)(2,1)} %param.15) | copy-start | bytes 786436
  25.2 5.0 %copy-start.6 = (bf16[512,512]{1,0:T(8,128)(2,1)S(1)}, bf16[512,512]{1,0:T(8,128)(2,1)}, u32[]{:S(2)}) copy-start(bf16[512,512]{1,0:T(8,128)(2,1)} %param.17) | copy-start | bytes 1572868
  25.2 5.0 %copy-start.8 = (f32[512]{0:T(512)S(1)}, f32[512]{0:T(512)}, u32[]{:S(2)}) copy-start(f32[512]{0:T(512)} %param.16) | copy-start | bytes 6148
  102.0 138.4 %all-reduce.5.cloned.1.call-start = ((), (), s32[]{:S(2)}) async-start(), calls=%async_computation.1 | async-start | bytes 1048576 | tf_op jit(solution)/shard_map/psum | solution.py:14
  110.5 31.7 %collective-permute-start = (bf16[3,128,1024]{2,1,0:T(8,128)(2,1)}, bf16[3,128,1024]{2,1,0:T(8,128)(2,1)S(1)}, u32[]{:S(2)}, u32[]{:S(2)}) collective-permute-start(bf16[3,128,1024]{2,1,0:T(8,128)(2,1)} %get-tuple-element.117), channel_id=1, source_target_pairs={{0,2},{2,4},{4,6},{6,8},{8,10},{10,12},{12,14},{1,3},{3,5},{5,7},{... | collective-permute-start | bytes 2359304 | tf_op jit(solution)/shard_map/ppermute | solution.py:25
  111.8 30.4 %collective-permute-start.1 = (bf16[3,128,1024]{2,1,0:T(8,128)(2,1)}, bf16[3,128,1024]{2,1,0:T(8,128)(2,1)}, u32[]{:S(2)}, u32[]{:S(2)}) collective-permute-start(bf16[3,128,1024]{2,1,0:T(8,128)(2,1)} %get-tuple-element.118), channel_id=1, source_target_pairs={{2,0},{4,2},{6,4},{8,6},{10,8},{12,10},{14,12},{3,1},{5,3},{7,5},{... | collective-permute-start | bytes 2359304 | tf_op jit(solution)/shard_map/ppermute | solution.py:26
  143.1 27.5 %collective-permute-start.2 = (bf16[14,3,1024]{2,1,0:T(4,128)(2,1)S(1)}, bf16[14,3,1024]{2,1,0:T(4,128)(2,1)S(1)}, u32[]{:S(2)}, u32[]{:S(2)}) collective-permute-start(bf16[14,3,1024]{2,1,0:T(4,128)(2,1)S(1)} %get-tuple-element.115), channel_id=1, source_target_pairs={{0,1},{2,3},{4,5},{6,7},{8,9},{10,11},{12,13},{14,15},{16,17},{18,... | collective-permute-start | bytes 258056 | tf_op jit(solution)/shard_map/ppermute | solution.py:25
  144.8 25.8 %collective-permute-start.3 = (bf16[14,3,1024]{2,1,0:T(4,128)(2,1)S(1)}, bf16[14,3,1024]{2,1,0:T(4,128)(2,1)S(1)}, u32[]{:S(2)}, u32[]{:S(2)}) collective-permute-start(bf16[14,3,1024]{2,1,0:T(4,128)(2,1)S(1)} %get-tuple-element.116), channel_id=1, source_target_pairs={{1,0},{3,2},{5,4},{7,6},{9,8},{11,10},{13,12},{15,14},{17,16},{19,... | collective-permute-start | bytes 258056 | tf_op jit(solution)/shard_map/ppermute | solution.py:26
  205.6 6.8 %copy-start.4 = (bf16[16,8,8,8,64]{4,3,2,0,1:T(8,128)(2,1)S(1)}, bf16[16,8,8,8,64]{4,3,2,0,1:T(8,128)(2,1)}, u32[]{:S(2)}) copy-start(bf16[16,8,8,8,64]{4,3,2,0,1:T(8,128)(2,1)} %fusion.30) | copy-start | bytes 3145732
  218.9 3.7 %copy-start.3 = (bf16[16,14,14,8,64]{4,3,1,2,0:T(8,128)(2,1)S(1)}, bf16[16,14,14,8,64]{4,3,1,2,0:T(8,128)(2,1)}, u32[]{:S(2)}) copy-start(bf16[16,14,14,8,64]{4,3,1,2,0:T(8,128)(2,1)} %copy.40) | copy-start | bytes 9633796
  228.6 13.9 %copy-start.1 = (bf16[512,1536]{1,0:T(8,128)(2,1)S(1)}, bf16[512,1536]{1,0:T(8,128)(2,1)}, u32[]{:S(2)}) copy-start(bf16[512,1536]{1,0:T(8,128)(2,1)} %param.13) | copy-start | bytes 4718596
  232.9 8.6 %copy-start.7 = (bf16[512,512]{1,0:T(8,128)(2,1)S(1)}, bf16[512,512]{1,0:T(8,128)(2,1)}, u32[]{:S(2)}) copy-start(bf16[512,512]{1,0:T(8,128)(2,1)} %param.18) | copy-start | bytes 1572868
Sparse Core Ops, SparseCore 0:
  102.2 15.9 all-reduce.2
  170.7 69.6 all-reduce.4
